TPU v7x, 512 devices: a whole 4x4x16 slice. The times are simulated.
512 devices in a mesh: head: 8 (over x, core), seq: 64 (over y, z).
Axes of the slice: x: 4, y: 4, z: 16, core: 2. Of those that a mesh axis runs over, the one named last changes fastest.
Arguments:
- queries: bfloat16 [32768, 4096], P('seq', 'head'), may hold values from -6 to 6
- keys: bfloat16 [32768, 4096], P('seq', 'head'), may hold values from -6 to 6
- values: bfloat16 [32768, 4096], P('seq', 'head'), may hold values from -6 to 6
- out_grad: bfloat16 [32768, 4096], P('seq', 'head'), may hold values from -8 to 8
- inputs: bfloat16 [32768, 2048], P('seq'), may hold values from -100 to 100
- momentum: float32 [2048, 4096], P('seq', 'head'), may hold values from -6 to 6
- level_weight: int32 [18, 32], replicated, may hold values from 1 to 8
Outputs:
- query_grad: bfloat16 [32768, 4096], P('seq', 'head')
- key_grad: bfloat16 [32768, 4096], P('seq', 'head')
- value_grad: bfloat16 [32768, 4096], P('seq', 'head')
- new_momentum: float32 [2048, 4096], P('seq', 'head')
All inputs are finite; a program needn't handle non-finite values.
Results may differ from a plain program's by a relative error of at most 0.0095.
Values may be sent and summed in bfloat16 or wider, within the bound.
No kernel may reach another device: no remote copies, remote signals or barrier semaphores. Data moves between devices by JAX's collectives and lax.ppermute only.
A program may use at most 64 MiB of HBM per device.

v0:
```python
import math
import jax
import jax.numpy as jnp
from jax import lax
from jax.sharding import Mesh
from jax.sharding import PartitionSpec as P

D_HEAD = 128
HEAD = ("head_0", "head_1")
SEQ = ("seq_0", "seq_1")
HEAD_SEQ = ("head_0", "head_1", "seq_0", "seq_1")
clip_norm = 1024.0
momentum_rate = 0.9


def partner(x, axis, apart):
    return lax.ppermute(x, axis, [(i, i ^ 1 << apart) for i in range(lax.axis_size(axis))])


def summed_rows(terms, axes):
    total = terms.astype(jnp.bfloat16)
    for axis in axes:
        total = lax.psum_scatter(total, axis, scatter_dimension=0, tiled=True)
    return total.astype(jnp.float32)


def by_axis(x, axes):
    for axis in axes:
        x = lax.psum(x, axis)
    return x


def bit_length(numbers, count):
    total = jnp.zeros_like(numbers)
    for place in range(count):
        total = total + (jnp.right_shift(numbers, place) > 0).astype(jnp.int32)
    return total


def level_table(level_weight, head_size):
    levels = jnp.arange(level_weight.shape[0], dtype=jnp.float32)
    factor = jnp.exp2(-0.5 * levels) / (8.0 * math.sqrt(head_size))
    return level_weight.astype(jnp.float32) * factor[:, None]


def lookup(level, table):
    onehot = (level[..., None] == jnp.arange(table.shape[0], dtype=jnp.int32)).astype(jnp.float32)
    flat = onehot.reshape(-1, table.shape[0])
    picked = jnp.dot(flat, table, precision=lax.Precision.HIGHEST)
    return picked.reshape(level.shape + (table.shape[1],))


def intra_weights(length, table):
    place = jnp.arange(length, dtype=jnp.int32)
    level = bit_length(jnp.bitwise_xor(place[:, None], place[None, :]), table.shape[0])
    picked = lookup(level, table)
    causal = (place[None, :] <= place[:, None])[..., None]
    return jnp.transpose(jnp.where(causal, picked, jnp.float32(0.0)), (2, 0, 1))


def local_grads(query, key_rows, value_rows, grad_rows, weights):
    scores = jnp.einsum("thd,shd->hts", query, key_rows, preferred_element_type=jnp.float32)
    mixed = (weights * scores).astype(jnp.bfloat16)
    value_part = jnp.einsum("hts,thd->shd", mixed, grad_rows, preferred_element_type=jnp.float32)
    before = jnp.einsum("thd,shd->hts", grad_rows, value_rows, preferred_element_type=jnp.float32)
    dmix = (weights * before).astype(jnp.bfloat16)
    query_part = jnp.einsum("hts,shd->thd", dmix, key_rows, preferred_element_type=jnp.float32)
    key_part = jnp.einsum("hts,thd->shd", dmix, query, preferred_element_type=jnp.float32)
    return (query_part, key_part, value_part)


def body(queries, keys, values, out_grad, inputs, momentum, level_weight):
    length = queries.shape[0]
    per_dev = queries.shape[1] // D_HEAD
    width = per_dev * D_HEAD
    table_all = level_table(level_weight, D_HEAD)
    table = lax.dynamic_slice_in_dim(table_all, lax.axis_index(HEAD) * per_dev, per_dev, 1)
    shape = (length, per_dev, D_HEAD)
    query = queries.reshape(shape)
    key_rows = keys.reshape(shape)
    value_rows = values.reshape(shape)
    grad_rows = out_grad.reshape(shape)
    states = jnp.einsum(
        "thd,the->hde", key_rows, value_rows, preferred_element_type=jnp.float32
    ).astype(jnp.bfloat16)
    grads = jnp.einsum("thd,the->hde", query, grad_rows, preferred_element_type=jnp.float32).astype(
        jnp.bfloat16
    )
    rank = lax.axis_index(SEQ)
    depth = lax.axis_size(SEQ).bit_length() - 1
    base_level = length.bit_length() - 1
    empty = jnp.zeros((per_dev, D_HEAD, D_HEAD), jnp.float32)
    block = (states.astype(jnp.float32), grads.astype(jnp.float32))
    state_sum = empty
    grad_sum = empty
    for bit in range(depth):
        other = (
            partner(block[0].astype(jnp.bfloat16), SEQ, bit).astype(jnp.float32),
            partner(block[1].astype(jnp.bfloat16), SEQ, bit).astype(jnp.float32),
        )
        weight = table[base_level + bit + 1][:, None, None]
        upper = jnp.bitwise_and(jnp.right_shift(rank, bit), 1) == 1
        state_sum = state_sum + jnp.where(upper, weight * other[0], jnp.float32(0.0))
        grad_sum = grad_sum + jnp.where(upper, jnp.float32(0.0), weight * other[1])
        block = (block[0] + other[0], block[1] + other[1])
    carried = state_sum.astype(jnp.bfloat16)
    returned = grad_sum.astype(jnp.bfloat16)
    weights = intra_weights(length, table)
    query_part, key_part, value_part = local_grads(query, key_rows, value_rows, grad_rows, weights)
    query_grad = query_part + jnp.einsum(
        "the,hde->thd", grad_rows, carried, preferred_element_type=jnp.float32
    )
    key_grad = key_part + jnp.einsum(
        "the,hde->thd", value_rows, returned, preferred_element_type=jnp.float32
    )
    value_grad = value_part + jnp.einsum(
        "thd,hde->the", key_rows, returned, preferred_element_type=jnp.float32
    )
    query_grad = query_grad.astype(jnp.bfloat16).reshape(length, width)
    key_grad = key_grad.astype(jnp.bfloat16).reshape(length, width)
    value_grad = value_grad.astype(jnp.bfloat16).reshape(length, width)
    shard = summed_rows(
        lax.dot_general(
            inputs, value_grad, (((0,), (0,)), ((), ())), preferred_element_type=jnp.float32
        ),
        SEQ,
    )
    total = by_axis(jnp.sum(shard * shard), HEAD_SEQ)
    factor = jnp.minimum(jnp.float32(1.0), clip_norm / jnp.sqrt(total + 1e-06))
    new_momentum = momentum_rate * momentum + factor * shard
    return (query_grad, key_grad, value_grad, new_momentum)


def solution(mesh):
    torus = Mesh(mesh.devices.reshape(4, 2, 4, 16), ("head_0", "head_1", "seq_0", "seq_1"))
    placed = (
        P(SEQ, HEAD),
        P(SEQ, HEAD),
        P(SEQ, HEAD),
        P(SEQ, HEAD),
        P(SEQ, None),
        P(SEQ, HEAD),
        P(),
    )
    return jax.shard_map(
        body,
        mesh=torus,
        in_specs=placed,
        out_specs=(P(SEQ, HEAD), P(SEQ, HEAD), P(SEQ, HEAD), P(SEQ, HEAD)),
        check_vma=False,
    )
```

profile of v0, /device:TPU:32, one launch (start us, length us, event | category | flops | bytes accessed | tf_op | source)
XLA Modules:
  0.0 279.5 jit_solution(11662807117163431342)
XLA Ops:
  7.2 0.0 reduce-scatter.5.cloned.1.call-start
  7.2 1.4 copy.110
  8.6 1.4 convolution_convert_fusion.1
  10.0 7.4 %collective-permute-start.6 = (bf16[4,128,128]{2,1,0:T(8,128)(2,1)S(1)}, bf16[4,128,128]{2,1,0:T(8,128)(2,1)S(1)}, u32[]{:S(2)}, u32[]{:S(2)}) collective-permute-start(bf16[4,128,128]{2,1,0:T(8,128)(2,1)S(1)} %convolution_convert_fusion.1), channel_id=1, source_target_pairs={{0,1},{1,0},{2,3},{3,2},{4,5},{5,4},{6,7},{7,6},{8,9},{9,8},{10,11... | collective-permute-start | bytes 393224 | tf_op jit(solution)/shard_map/ppermute | solution.py:17
  17.4 2.9 %collective-permute-done.6 = bf16[4,128,128]{2,1,0:T(8,128)(2,1)S(1)} collective-permute-done((bf16[4,128,128]{2,1,0:T(8,128)(2,1)S(1)}, bf16[4,128,128]{2,1,0:T(8,128)(2,1)S(1)}, u32[]{:S(2)}, u32[]{:S(2)}) %collective-permute-start.6) | collective-permute-done | bytes 131104 | tf_op jit(solution)/shard_map/ppermute | solution.py:17
  20.4 0.7 fusion.62
  21.0 2.0 collective-permute-start.7
  23.0 3.3 %convert_add_fusion = s32[512,512]{1,0:T(8,128)} fusion(), kind=kLoop, calls=%fused_computation.23 | loop fusion | flops 18874368 | bytes 1048576 | tf_op jit(solution)/shard_map/add | solution.py:36
  26.4 2.7 collective-permute-done.7
  29.1 0.1 fusion.86
  29.2 7.9 %collective-permute-start.8 = (bf16[4,128,128]{2,1,0:T(8,128)(2,1)S(1)}, bf16[4,128,128]{2,1,0:T(8,128)(2,1)S(1)}, u32[]{:S(2)}, u32[]{:S(2)}) collective-permute-start(bf16[4,128,128]{2,1,0:T(8,128)(2,1)S(1)} %fusion.86), channel_id=1, source_target_pairs={{0,4},{1,5},{2,6},{3,7},{4,0},{5,1},{6,2},{7,3},{8,12},{9,13},{10,... | collective-permute-start | bytes 393224 | tf_op jit(solution)/shard_map/ppermute | solution.py:17
  37.1 0.8 fusion.81
  37.9 6.7 %collective-permute-done.8 = bf16[4,128,128]{2,1,0:T(8,128)(2,1)S(1)} collective-permute-done((bf16[4,128,128]{2,1,0:T(8,128)(2,1)S(1)}, bf16[4,128,128]{2,1,0:T(8,128)(2,1)S(1)}, u32[]{:S(2)}, u32[]{:S(2)}) %collective-permute-start.8) | collective-permute-done | bytes 131104 | tf_op jit(solution)/shard_map/ppermute | solution.py:17
  44.6 0.1 fusion.64
  44.7 12.8 %collective-permute-start.9 = (bf16[4,128,128]{2,1,0:T(8,128)(2,1)S(1)}, bf16[4,128,128]{2,1,0:T(8,128)(2,1)S(1)}, u32[]{:S(2)}, u32[]{:S(2)}) collective-permute-start(bf16[4,128,128]{2,1,0:T(8,128)(2,1)S(1)} %fusion.64), channel_id=1, source_target_pairs={{0,8},{1,9},{2,10},{3,11},{4,12},{5,13},{6,14},{7,15},{8,0},{9,1},... | collective-permute-start | bytes 393224 | tf_op jit(solution)/shard_map/ppermute | solution.py:17
  57.6 10.5 %fusion = f32[4,512,512]{2,0,1:T(4,128)} fusion(s32[512,512]{1,0:T(8,128)} %convert_add_fusion, f32[18,4]{1,0:T(8,128)S(1)} %fusion.81), kind=kOutput, calls=%fused_computation.1 | convolution fusion | flops 231211008 | bytes 5243168 | tf_op jit(solution)/shard_map/dot_general | solution.py:49
  68.1 0.8 iota_compare_fusion.2
  68.9 0.7 fusion.80
  69.6 3.5 %collective-permute-start.10 = (bf16[4,128,128]{2,1,0:T(8,128)(2,1)}, bf16[4,128,128]{2,1,0:T(8,128)(2,1)}, u32[]{:S(2)}, u32[]{:S(2)}) collective-permute-start(bf16[4,128,128]{2,1,0:T(8,128)(2,1)} %fusion.80), channel_id=1, source_target_pairs={{0,16},{1,17},{2,18},{3,19},{4,20},{5,21},{6,22},{7,23},{8,24},{9,... | collective-permute-start | bytes 393224 | tf_op jit(solution)/shard_map/ppermute | solution.py:17
  73.1 5.7 %fusion.4 = f32[512,4,128]{0,2,1:T(8,128)} fusion(bf16[512,4,128]{0,2,1:T(8,128)(2,1)S(1)} %bitcast.115, f32[4,512,512]{2,0,1:T(4,128)} %fusion, pred[512,512]{1,0:T(8,128)(4,1)} %iota_compare_fusion.2, bf16[512,512]{1,0:T(8,128)(2,1)} %param.7, bf16[512,512]{1,0:T(8,128)(2,1)S(1)} %copy-done.2), kind=kOutput, calls=%fused_computation.11 | convolution fusion | flops 540016640 | bytes 7077888 | tf_op jit(solution)/shard_map/hts,thd->shd/dot_general | solution.py:64
  78.8 1.1 fusion.58
  79.9 5.0 %collective-permute-start.11 = (bf16[4,128,128]{2,1,0:T(8,128)(2,1)S(1)}, bf16[4,128,128]{2,1,0:T(8,128)(2,1)S(1)}, u32[]{:S(2)}, u32[]{:S(2)}) collective-permute-start(bf16[4,128,128]{2,1,0:T(8,128)(2,1)S(1)} %fusion.58), channel_id=1, source_target_pairs={{0,32},{1,33},{2,34},{3,35},{4,36},{5,37},{6,38},{7,39},{8,40},{9,... | collective-permute-start | bytes 393224 | tf_op jit(solution)/shard_map/ppermute | solution.py:17
  85.0 3.3 %collective-permute-done.11 = bf16[4,128,128]{2,1,0:T(8,128)(2,1)S(1)} collective-permute-done((bf16[4,128,128]{2,1,0:T(8,128)(2,1)S(1)}, bf16[4,128,128]{2,1,0:T(8,128)(2,1)S(1)}, u32[]{:S(2)}, u32[]{:S(2)}) %collective-permute-start.11) | collective-permute-done | bytes 131104 | tf_op jit(solution)/shard_map/ppermute | solution.py:17
  88.3 0.7 copy-done.11
  89.0 2.0 fusion.10
  91.0 0.8 copy-done.7
  91.8 2.6 fusion.2
  94.4 0.0 reduce-scatter.5.cloned.1.call-update
  94.4 0.0 reduce-scatter.7.cloned.1.call-start
  94.5 1.4 convolution_convert_fusion.2
  95.9 6.7 %collective-permute-start = (bf16[4,128,128]{2,1,0:T(8,128)(2,1)S(1)}, bf16[4,128,128]{2,1,0:T(8,128)(2,1)S(1)}, u32[]{:S(2)}, u32[]{:S(2)}) collective-permute-start(bf16[4,128,128]{2,1,0:T(8,128)(2,1)S(1)} %convolution_convert_fusion.2), channel_id=1, source_target_pairs={{0,1},{1,0},{2,3},{3,2},{4,5},{5,4},{6,7},{7,6},{8,9},{9,8},{10,11... | collective-permute-start | bytes 393224 | tf_op jit(solution)/shard_map/ppermute | solution.py:17
  102.6 2.9 %collective-permute-done = bf16[4,128,128]{2,1,0:T(8,128)(2,1)S(1)} collective-permute-done((bf16[4,128,128]{2,1,0:T(8,128)(2,1)S(1)}, bf16[4,128,128]{2,1,0:T(8,128)(2,1)S(1)}, u32[]{:S(2)}, u32[]{:S(2)}) %collective-permute-start) | collective-permute-done | bytes 131104 | tf_op jit(solution)/shard_map/ppermute | solution.py:17
  105.6 1.9 collective-permute-start.1
  107.5 5.9 %collective-permute-done.1 = bf16[4,128,128]{2,1,0:T(8,128)(2,1)S(1)} collective-permute-done((bf16[4,128,128]{2,1,0:T(8,128)(2,1)S(1)}, bf16[4,128,128]{2,1,0:T(8,128)(2,1)S(1)}, u32[]{:S(2)}, u32[]{:S(2)}) %collective-permute-start.1) | collective-permute-done | bytes 131104 | tf_op jit(solution)/shard_map/ppermute | solution.py:17
  113.5 0.1 fusion.85
  113.5 6.9 %collective-permute-start.2 = (bf16[4,128,128]{2,1,0:T(8,128)(2,1)S(1)}, bf16[4,128,128]{2,1,0:T(8,128)(2,1)S(1)}, u32[]{:S(2)}, u32[]{:S(2)}) collective-permute-start(bf16[4,128,128]{2,1,0:T(8,128)(2,1)S(1)} %fusion.85), channel_id=1, source_target_pairs={{0,4},{1,5},{2,6},{3,7},{4,0},{5,1},{6,2},{7,3},{8,12},{9,13},{10,... | collective-permute-start | bytes 393224 | tf_op jit(solution)/shard_map/ppermute | solution.py:17
  120.4 4.2 %multiply_convert_fusion.1 = bf16[4,512,512]{2,1,0:T(8,128)(2,1)S(1)} fusion(f32[4,512,512]{2,0,1:T(4,128)} %fusion, bf16[512,4,128]{0,2,1:T(8,128)(2,1)S(1)} %bitcast.116, pred[512,512]{1,0:T(8,128)(4,1)} %iota_compare_fusion.2, bf16[512,512]{1,0:T(8,128)(2,1)} %param.9), kind=kOutput, calls=%fused_computation.5 | convolution fusion | flops 271581184 | bytes 7602176 | tf_op jit(solution)/shard_map/thd,shd->hts/dot_general | solution.py:65
  124.6 2.6 collective-permute-done.2
  127.2 0.7 fusion.63
  128.0 5.5 %collective-permute-start.3 = (bf16[4,128,128]{2,1,0:T(8,128)(2,1)}, bf16[4,128,128]{2,1,0:T(8,128)(2,1)}, u32[]{:S(2)}, u32[]{:S(2)}) collective-permute-start(bf16[4,128,128]{2,1,0:T(8,128)(2,1)} %fusion.63), channel_id=1, source_target_pairs={{0,8},{1,9},{2,10},{3,11},{4,12},{5,13},{6,14},{7,15},{8,0},{9,1},... | collective-permute-start | bytes 393224 | tf_op jit(solution)/shard_map/ppermute | solution.py:17
  133.5 1.5 convolution_bitcast_fusion
  135.0 2.0 copy.108
  137.1 7.4 %collective-permute-done.3 = bf16[4,128,128]{2,1,0:T(8,128)(2,1)} collective-permute-done((bf16[4,128,128]{2,1,0:T(8,128)(2,1)}, bf16[4,128,128]{2,1,0:T(8,128)(2,1)}, u32[]{:S(2)}, u32[]{:S(2)}) %collective-permute-start.3) | collective-permute-done | bytes 131104 | tf_op jit(solution)/shard_map/ppermute | solution.py:17
  144.5 1.8 fusion.79
  146.3 1.9 collective-permute-start.4
  148.2 3.4 %convolution_bitcast_fusion.1 = f32[512,4,128]{0,2,1:T(8,128)} fusion(bf16[4,512,512]{2,1,0:T(8,128)(2,1)} %copy-done.1, bf16[512,512]{1,0:T(8,128)(2,1)S(1)} %copy-done.2), kind=kOutput, calls=%fused_computation.10 | convolution fusion | flops 268435456 | bytes 3670016 | tf_op jit(solution)/shard_map/hts,shd->thd/dot_general | solution.py:67
  151.6 1.7 copy.100
  153.3 0.1 collective-permute-done.4
  153.5 1.9 fusion.46
  155.4 5.0 %collective-permute-start.5 = (bf16[4,128,128]{2,1,0:T(8,128)(2,1)}, bf16[4,128,128]{2,1,0:T(8,128)(2,1)}, u32[]{:S(2)}, u32[]{:S(2)}) collective-permute-start(bf16[4,128,128]{2,1,0:T(8,128)(2,1)} %fusion.46), channel_id=1, source_target_pairs={{0,32},{1,33},{2,34},{3,35},{4,36},{5,37},{6,38},{7,39},{8,40},{9,... | collective-permute-start | bytes 393224 | tf_op jit(solution)/shard_map/ppermute | solution.py:17
  160.5 2.9 %fusion.9 = bf16[512,4,128]{0,2,1:T(8,128)(2,1)} fusion(f32[512,4,128]{0,2,1:T(8,128)} %convolution_bitcast_fusion, bf16[4,128,128]{2,1,0:T(8,128)(2,1)S(1)} %collective-permute-done.6, bf16[4,128,128]{2,1,0:T(8,128)(2,1)S(1)} %collective-permute-done.7, bf16[4,128,128]{2,1,0:T(8,128)(2,1)} %copy-done.4, bf16[4,128,128]{2,1,0:T(8,128)(2,1)} %copy-done.9, ...), kind=kOutput, calls=%fused_computation.19 | convolution fusion | flops 69206016 | bytes 2883686 | tf_op jit(solution)/shard_map/the,hde->thd/dot_general | solution.py:113
  163.4 43.5 %reduce-scatter.7.cloned.1.call-done = bf16[32,512]{1,0:T(8,128)(2,1)} async-done(((bf16[512,512]{1,0:T(8,128)(2,1)}), bf16[32,512]{1,0:T(8,128)(2,1)}) %reduce-scatter.7.cloned.1.call-update) | async-done | bytes 32784
  206.8 0.9 copy.109
  207.7 0.7 fusion.59
  208.4 2.8 fusion.8
  211.2 11.2 %psum.28 = f32[]{:T(128)} all-reduce(f32[]{:T(128)} %fusion.59), channel_id=1, replica_groups=mesh['head_0'=4,'head_1'=2,'seq_0'=4,'seq_1'=16] {'head_0'}, use_global_device_ids=true, to_apply=%region_3.4 | all-reduce | flops 1 | bytes 8 | tf_op jit(solution)/shard_map/psum | solution.py:29
  222.4 1.0 copy.103
  223.4 3.1 %psum.29 = f32[]{:T(128)} all-reduce(f32[]{:T(128)} %psum.28), channel_id=1, replica_groups=mesh['head_0'=4,'head_1'=2,'seq_0'=4,'seq_1'=16] {'head_1'}, use_global_device_ids=true, to_apply=%region_4.5 | all-reduce | flops 1 | bytes 8 | tf_op jit(solution)/shard_map/psum | solution.py:29
  226.4 2.0 copy.102
  228.5 11.0 %psum.30 = f32[]{:T(128)} all-reduce(f32[]{:T(128)} %psum.29), channel_id=1, replica_groups=mesh['head_0'=4,'head_1'=2,'seq_0'=4,'seq_1'=16] {'seq_0'}, use_global_device_ids=true, to_apply=%region_5.6 | all-reduce | flops 1 | bytes 8 | tf_op jit(solution)/shard_map/psum | solution.py:29
  239.5 2.0 copy.101
  241.6 28.7 %psum.31 = f32[]{:T(128)} all-reduce(f32[]{:T(128)} %psum.30), channel_id=1, replica_groups=mesh['head_0'=4,'head_1'=2,'seq_0'=4,'seq_1'=16] {'seq_1'}, use_global_device_ids=true, to_apply=%region_6.7 | all-reduce | flops 1 | bytes 8 | tf_op jit(solution)/shard_map/psum | solution.py:29
  271.0 1.0 fusion.60
  271.9 0.7 copy.104
  (46 shorter events, 0.2 us)
Async XLA Ops:
  7.2 84.6 %copy-start = (bf16[512,2048]{1,0:T(8,128)(2,1)S(1)}, bf16[512,2048]{1,0:T(8,128)(2,1)}, u32[]{:S(2)}) copy-start(bf16[512,2048]{1,0:T(8,128)(2,1)} %param.11) | copy-start | bytes 6291460
  7.2 127.8 %reduce-scatter.5.cloned.1.call-start = ((), (), s32[]{:S(2)}) async-start(), calls=%async_computation.2 | async-start | bytes 2621440 | tf_op jit(solution)/shard_map/reduce_scatter | solution.py:23
  10.0 10.3 %collective-permute-start.6 = (bf16[4,128,128]{2,1,0:T(8,128)(2,1)S(1)}, bf16[4,128,128]{2,1,0:T(8,128)(2,1)S(1)}, u32[]{:S(2)}, u32[]{:S(2)}) collective-permute-start(bf16[4,128,128]{2,1,0:T(8,128)(2,1)S(1)} %convolution_convert_fusion.1), channel_id=1, source_target_pairs={{0,1},{1,0},{2,3},{3,2},{4,5},{5,4},{6,7},{7,6},{8,9},{9,8},{10,11... | collective-permute-start | bytes 393224 | tf_op jit(solution)/shard_map/ppermute | solution.py:17
  21.0 8.1 %collective-permute-start.7 = (bf16[4,128,128]{2,1,0:T(8,128)(2,1)}, bf16[4,128,128]{2,1,0:T(8,128)(2,1)S(1)}, u32[]{:S(2)}, u32[]{:S(2)}) collective-permute-start(bf16[4,128,128]{2,1,0:T(8,128)(2,1)} %fusion.62), channel_id=1, source_target_pairs={{0,2},{1,3},{2,0},{3,1},{4,6},{5,7},{6,4},{7,5},{8,10},{9,11},{10,... | collective-permute-start | bytes 393224 | tf_op jit(solution)/shard_map/ppermute | solution.py:17
  26.4 46.8 %copy-start.2 = (bf16[512,512]{1,0:T(8,128)(2,1)S(1)}, bf16[512,512]{1,0:T(8,128)(2,1)}, u32[]{:S(2)}) copy-start(bf16[512,512]{1,0:T(8,128)(2,1)} %param.8) | copy-start | bytes 1572868
  29.2 15.5 %collective-permute-start.8 = (bf16[4,128,128]{2,1,0:T(8,128)(2,1)S(1)}, bf16[4,128,128]{2,1,0:T(8,128)(2,1)S(1)}, u32[]{:S(2)}, u32[]{:S(2)}) collective-permute-start(bf16[4,128,128]{2,1,0:T(8,128)(2,1)S(1)} %fusion.86), channel_id=1, source_target_pairs={{0,4},{1,5},{2,6},{3,7},{4,0},{5,1},{6,2},{7,3},{8,12},{9,13},{10,... | collective-permute-start | bytes 393224 | tf_op jit(solution)/shard_map/ppermute | solution.py:17
  44.6 24.3 %copy-start.4 = (bf16[4,128,128]{2,1,0:T(8,128)(2,1)}, bf16[4,128,128]{2,1,0:T(8,128)(2,1)S(1)}, u32[]{:S(2)}) copy-start(bf16[4,128,128]{2,1,0:T(8,128)(2,1)S(1)} %collective-permute-done.8) | copy-start | bytes 393220
  44.7 24.2 %collective-permute-start.9 = (bf16[4,128,128]{2,1,0:T(8,128)(2,1)S(1)}, bf16[4,128,128]{2,1,0:T(8,128)(2,1)S(1)}, u32[]{:S(2)}, u32[]{:S(2)}) collective-permute-start(bf16[4,128,128]{2,1,0:T(8,128)(2,1)S(1)} %fusion.64), channel_id=1, source_target_pairs={{0,8},{1,9},{2,10},{3,11},{4,12},{5,13},{6,14},{7,15},{8,0},{9,1},... | collective-permute-start | bytes 393224 | tf_op jit(solution)/shard_map/ppermute | solution.py:17
  68.9 0.8 copy-start.9
  69.6 9.2 %collective-permute-start.10 = (bf16[4,128,128]{2,1,0:T(8,128)(2,1)}, bf16[4,128,128]{2,1,0:T(8,128)(2,1)}, u32[]{:S(2)}, u32[]{:S(2)}) collective-permute-start(bf16[4,128,128]{2,1,0:T(8,128)(2,1)} %fusion.80), channel_id=1, source_target_pairs={{0,16},{1,17},{2,18},{3,19},{4,20},{5,21},{6,22},{7,23},{8,24},{9,... | collective-permute-start | bytes 393224 | tf_op jit(solution)/shard_map/ppermute | solution.py:17
  79.9 8.4 %collective-permute-start.11 = (bf16[4,128,128]{2,1,0:T(8,128)(2,1)S(1)}, bf16[4,128,128]{2,1,0:T(8,128)(2,1)S(1)}, u32[]{:S(2)}, u32[]{:S(2)}) collective-permute-start(bf16[4,128,128]{2,1,0:T(8,128)(2,1)S(1)} %fusion.58), channel_id=1, source_target_pairs={{0,32},{1,33},{2,34},{3,35},{4,36},{5,37},{6,38},{7,39},{8,40},{9,... | collective-permute-start | bytes 393224 | tf_op jit(solution)/shard_map/ppermute | solution.py:17
  85.0 6.0 %copy-start.12 = (f32[4]{0:T(128)}, f32[4]{0:T(128)S(1)}, u32[]{:S(2)}) copy-start(f32[4]{0:T(128)S(1)} %get-tuple-element.21) | copy-start | bytes 52
  85.0 6.0 %copy-start.14 = (f32[4]{0:T(128)}, f32[4]{0:T(128)S(1)}, u32[]{:S(2)}) copy-start(f32[4]{0:T(128)S(1)} %get-tuple-element.22) | copy-start | bytes 52
  85.0 6.0 %copy-start.16 = (f32[4]{0:T(128)}, f32[4]{0:T(128)S(1)}, u32[]{:S(2)}) copy-start(f32[4]{0:T(128)S(1)} %get-tuple-element.23) | copy-start | bytes 52
  85.0 6.0 %copy-start.18 = (f32[4]{0:T(128)}, f32[4]{0:T(128)S(1)}, u32[]{:S(2)}) copy-start(f32[4]{0:T(128)S(1)} %get-tuple-element.24) | copy-start | bytes 52
  85.0 6.0 %copy-start.19 = (f32[4]{0:T(128)}, f32[4]{0:T(128)S(1)}, u32[]{:S(2)}) copy-start(f32[4]{0:T(128)S(1)} %get-tuple-element.25) | copy-start | bytes 52
  88.3 0.7 copy-start.11
  91.0 0.8 copy-start.7
  94.4 112.4 %reduce-scatter.7.cloned.1.call-start = ((), (), s32[]{:S(2)}) async-start(), calls=%async_computation.3 | async-start | bytes 557056
  95.9 31.4 %copy-start.6 = (bf16[4,128,128]{2,1,0:T(8,128)(2,1)}, bf16[4,128,128]{2,1,0:T(8,128)(2,1)S(1)}, u32[]{:S(2)}) copy-start(bf16[4,128,128]{2,1,0:T(8,128)(2,1)S(1)} %convolution_convert_fusion.2) | copy-start | bytes 393220
  95.9 9.7 %collective-permute-start = (bf16[4,128,128]{2,1,0:T(8,128)(2,1)S(1)}, bf16[4,128,128]{2,1,0:T(8,128)(2,1)S(1)}, u32[]{:S(2)}, u32[]{:S(2)}) collective-permute-start(bf16[4,128,128]{2,1,0:T(8,128)(2,1)S(1)} %convolution_convert_fusion.2), channel_id=1, source_target_pairs={{0,1},{1,0},{2,3},{3,2},{4,5},{5,4},{6,7},{7,6},{8,9},{9,8},{10,11... | collective-permute-start | bytes 393224 | tf_op jit(solution)/shard_map/ppermute | solution.py:17
  105.6 7.9 %collective-permute-start.1 = (bf16[4,128,128]{2,1,0:T(8,128)(2,1)S(1)}, bf16[4,128,128]{2,1,0:T(8,128)(2,1)S(1)}, u32[]{:S(2)}, u32[]{:S(2)}) collective-permute-start(bf16[4,128,128]{2,1,0:T(8,128)(2,1)S(1)} %fusion.61), channel_id=1, source_target_pairs={{0,2},{1,3},{2,0},{3,1},{4,6},{5,7},{6,4},{7,5},{8,10},{9,11},{10,... | collective-permute-start | bytes 393224 | tf_op jit(solution)/shard_map/ppermute | solution.py:17
  113.5 14.5 %copy-start.5 = (bf16[4,128,128]{2,1,0:T(8,128)(2,1)}, bf16[4,128,128]{2,1,0:T(8,128)(2,1)S(1)}, u32[]{:S(2)}) copy-start(bf16[4,128,128]{2,1,0:T(8,128)(2,1)S(1)} %collective-permute-done.1) | copy-start | bytes 393220
  113.5 20.0 %copy-start.3 = (bf16[512,512]{1,0:T(8,128)(2,1)S(1)}, bf16[512,512]{1,0:T(8,128)(2,1)}, u32[]{:S(2)}) copy-start(bf16[512,512]{1,0:T(8,128)(2,1)} %param.7) | copy-start | bytes 1572868
  113.5 13.7 %collective-permute-start.2 = (bf16[4,128,128]{2,1,0:T(8,128)(2,1)S(1)}, bf16[4,128,128]{2,1,0:T(8,128)(2,1)S(1)}, u32[]{:S(2)}, u32[]{:S(2)}) collective-permute-start(bf16[4,128,128]{2,1,0:T(8,128)(2,1)S(1)} %fusion.85), channel_id=1, source_target_pairs={{0,4},{1,5},{2,6},{3,7},{4,0},{5,1},{6,2},{7,3},{8,12},{9,13},{10,... | collective-permute-start | bytes 393224 | tf_op jit(solution)/shard_map/ppermute | solution.py:17
  124.6 8.9 %copy-start.1 = (bf16[4,512,512]{2,1,0:T(8,128)(2,1)}, bf16[4,512,512]{2,1,0:T(8,128)(2,1)S(1)}, u32[]{:S(2)}) copy-start(bf16[4,512,512]{2,1,0:T(8,128)(2,1)S(1)} %multiply_convert_fusion.1) | copy-start | bytes 6291460
  127.2 6.3 %copy-start.10 = (bf16[4,128,128]{2,1,0:T(8,128)(2,1)}, bf16[4,128,128]{2,1,0:T(8,128)(2,1)S(1)}, u32[]{:S(2)}) copy-start(bf16[4,128,128]{2,1,0:T(8,128)(2,1)S(1)} %collective-permute-done.2) | copy-start | bytes 393220
  128.0 16.5 %collective-permute-start.3 = (bf16[4,128,128]{2,1,0:T(8,128)(2,1)}, bf16[4,128,128]{2,1,0:T(8,128)(2,1)}, u32[]{:S(2)}, u32[]{:S(2)}) collective-permute-start(bf16[4,128,128]{2,1,0:T(8,128)(2,1)} %fusion.63), channel_id=1, source_target_pairs={{0,8},{1,9},{2,10},{3,11},{4,12},{5,13},{6,14},{7,15},{8,0},{9,1},... | collective-permute-start | bytes 393224 | tf_op jit(solution)/shard_map/ppermute | solution.py:17
  135.0 25.4 %copy-start.13 = (f32[4]{0:T(128)S(1)}, f32[4]{0:T(128)}, u32[]{:S(2)}) copy-start(f32[4]{0:T(128)} %copy-done.12) | copy-start | bytes 52
  135.0 25.4 %copy-start.15 = (f32[4]{0:T(128)S(1)}, f32[4]{0:T(128)}, u32[]{:S(2)}) copy-start(f32[4]{0:T(128)} %copy-done.14) | copy-start | bytes 52
  135.0 25.4 %copy-start.17 = (f32[4]{0:T(128)S(1)}, f32[4]{0:T(128)}, u32[]{:S(2)}) copy-start(f32[4]{0:T(128)} %copy-done.16) | copy-start | bytes 52
  146.3 7.2 %collective-permute-start.4 = (bf16[4,128,128]{2,1,0:T(8,128)(2,1)}, bf16[4,128,128]{2,1,0:T(8,128)(2,1)}, u32[]{:S(2)}, u32[]{:S(2)}) collective-permute-start(bf16[4,128,128]{2,1,0:T(8,128)(2,1)} %fusion.79), channel_id=1, source_target_pairs={{0,16},{1,17},{2,18},{3,19},{4,20},{5,21},{6,22},{7,23},{8,24},{9,... | collective-permute-start | bytes 393224 | tf_op jit(solution)/shard_map/ppermute | solution.py:17
  151.6 70.8 %copy-start.8 = (bf16[512,4,128]{0,2,1:T(8,128)(2,1)S(1)}, bf16[512,4,128]{0,2,1:T(8,128)(2,1)}, u32[]{:S(2)}) copy-start(bf16[512,4,128]{0,2,1:T(8,128)(2,1)} %copy-done.7) | copy-start | bytes 1572868
  155.4 53.0 %collective-permute-start.5 = (bf16[4,128,128]{2,1,0:T(8,128)(2,1)}, bf16[4,128,128]{2,1,0:T(8,128)(2,1)}, u32[]{:S(2)}, u32[]{:S(2)}) collective-permute-start(bf16[4,128,128]{2,1,0:T(8,128)(2,1)} %fusion.46), channel_id=1, source_target_pairs={{0,32},{1,33},{2,34},{3,35},{4,36},{5,37},{6,38},{7,39},{8,40},{9,... | collective-permute-start | bytes 393224 | tf_op jit(solution)/shard_map/ppermute | solution.py:17
Sparse Core Ops, SparseCore 0:
  94.6 38.4 reduce-scatter.4
  137.2 69.5 reduce-scatter.6
where the time goes:
time: 281 us; the launch traced here: 280 us
  waiting for transfers between devices  78.2 us (28%)
  starting transfers between devices  66.6 us (24%)
  blocking collectives  54 us (19%)
  matrix products  38.3 us (14%)
  between operations  15.1 us (5%)
  other arithmetic  13.9 us (5%)
  local copies, waits for them, and re-layouts  13.4 us (5%)
    ppermute x12, starting transfers between devices, partner(): lax.ppermute(x, axis, [(i, i ^ 1 << apart) for i in range(lax.axis_size(a...  66.5 us
    psum x4, blocking collectives, by_axis(): x = lax.psum(x, axis)  54 us
    unnamed x3, waiting for transfers between devices  43.5 us
    ppermute x12, waiting for transfers between devices, partner(): lax.ppermute(x, axis, [(i, i ^ 1 << apart) for i in range(lax.axis_size(a...  34.7 us
    unnamed x47, local copies, waits for them, and re-layouts  12 us
    dot_general x1, matrix products, lookup(): picked = jnp.dot(flat, table, precision=lax.Precision.HIGHEST)  10.5 us
    dot_general x1, matrix products, local_grads(): jnp.einsum('hts,thd->shd', mixed, grad_rows, preferred_element_type=jnp.f...  5.68 us
  transfers between devices with their start and end apart: 14, of which 10 were waited for; matrix products, arithmetic and copies ran while one was open for 16% of the time, Pallas kernels for 0%

commit v1 on v0

--- a/solution.py
+++ b/solution.py
@@ -26,7 +26,7 @@
 
 def by_axis(x, axes):
     for axis in axes:
-        x = lax.psum(x, axis)
+        x = jnp.sum(lax.all_gather(x, axis), axis=0)
     return x
 
 

time: 281 us -> 300 us (1.068)
  local copies, waits for them, and re-layouts: 13.4 us -> 25 us
  waiting for transfers between devices: 78.2 us -> 88.2 us
    psum x4 -> x0, blocking collectives: 54 us -> none  [by_axis(): x = lax.psum(x, axis)]
    unnamed x0 -> x4, blocking collectives: none -> 51.3 us
    unnamed x47 -> x67, local copies, waits for them, and re-layouts: 12 us -> 23.6 us
    unnamed x3, waiting for transfers between devices: 43.5 us -> 51.5 us
where the time goes in v1:
time: 300 us; the launch traced here: 298 us
  waiting for transfers between devices  88.2 us (29%)
  starting transfers between devices  67.2 us (22%)
  blocking collectives  51.3 us (17%)
  matrix products  37.6 us (13%)
  local copies, waits for them, and re-layouts  25 us (8%)
  between operations  15.1 us (5%)
  other arithmetic  14 us (5%)
    ppermute x12, starting transfers between devices, partner(): lax.ppermute(x, axis, [(i, i ^ 1 << apart) for i in range(lax.axis_size(a...  67.1 us
    unnamed x3, waiting for transfers between devices  51.5 us
    unnamed x4, blocking collectives  51.3 us
    ppermute x12, waiting for transfers between devices, partner(): lax.ppermute(x, axis, [(i, i ^ 1 << apart) for i in range(lax.axis_size(a...  36.7 us
    unnamed x67, local copies, waits for them, and re-layouts  23.6 us
    dot_general x1, matrix products, lookup(): picked = jnp.dot(flat, table, precision=lax.Precision.HIGHEST)  10.6 us
  transfers between devices with their start and end apart: 14, of which 10 were waited for; matrix products, arithmetic and copies ran while one was open for 16% of the time, Pallas kernels for 0%

profile of v1, /device:TPU:32, one launch (start us, length us, event | category | flops | bytes accessed | tf_op | source)
XLA Modules:
  0.0 298.4 jit_solution(10957868018756400359)
XLA Ops:
  7.2 1.4 copy.110
  8.6 1.4 convolution_convert_fusion.1
  10.0 7.4 %collective-permute-start.6 = (bf16[4,128,128]{2,1,0:T(8,128)(2,1)S(1)}, bf16[4,128,128]{2,1,0:T(8,128)(2,1)S(1)}, u32[]{:S(2)}, u32[]{:S(2)}) collective-permute-start(bf16[4,128,128]{2,1,0:T(8,128)(2,1)S(1)} %convolution_convert_fusion.1), channel_id=1, source_target_pairs={{0,1},{1,0},{2,3},{3,2},{4,5},{5,4},{6,7},{7,6},{8,9},{9,8},{10,11... | collective-permute-start | bytes 393224 | tf_op jit(solution)/shard_map/ppermute | solution.py:17
  17.4 2.9 collective-permute-done.6
  20.4 0.7 fusion.62
  21.0 2.0 collective-permute-start.7
  23.0 3.3 %convert_add_fusion = s32[512,512]{1,0:T(8,128)} fusion(), kind=kLoop, calls=%fused_computation.23 | loop fusion | flops 18874368 | bytes 1048576 | tf_op jit(solution)/shard_map/add | solution.py:36
  26.4 2.7 collective-permute-done.7
  29.2 7.9 %collective-permute-start.8 = (bf16[4,128,128]{2,1,0:T(8,128)(2,1)S(1)}, bf16[4,128,128]{2,1,0:T(8,128)(2,1)S(1)}, u32[]{:S(2)}, u32[]{:S(2)}) collective-permute-start(bf16[4,128,128]{2,1,0:T(8,128)(2,1)S(1)} %fusion.86), channel_id=1, source_target_pairs={{0,4},{1,5},{2,6},{3,7},{4,0},{5,1},{6,2},{7,3},{8,12},{9,13},{10,... | collective-permute-start | bytes 393224 | tf_op jit(solution)/shard_map/ppermute | solution.py:17
  37.1 0.8 fusion.81
  37.9 6.7 %collective-permute-done.8 = bf16[4,128,128]{2,1,0:T(8,128)(2,1)S(1)} collective-permute-done((bf16[4,128,128]{2,1,0:T(8,128)(2,1)S(1)}, bf16[4,128,128]{2,1,0:T(8,128)(2,1)S(1)}, u32[]{:S(2)}, u32[]{:S(2)}) %collective-permute-start.8) | collective-permute-done | bytes 131104 | tf_op jit(solution)/shard_map/ppermute | solution.py:17
  44.7 12.8 %collective-permute-start.9 = (bf16[4,128,128]{2,1,0:T(8,128)(2,1)S(1)}, bf16[4,128,128]{2,1,0:T(8,128)(2,1)S(1)}, u32[]{:S(2)}, u32[]{:S(2)}) collective-permute-start(bf16[4,128,128]{2,1,0:T(8,128)(2,1)S(1)} %fusion.64), channel_id=1, source_target_pairs={{0,8},{1,9},{2,10},{3,11},{4,12},{5,13},{6,14},{7,15},{8,0},{9,1},... | collective-permute-start | bytes 393224 | tf_op jit(solution)/shard_map/ppermute | solution.py:17
  57.6 10.6 %fusion = f32[4,512,512]{2,0,1:T(4,128)} fusion(s32[512,512]{1,0:T(8,128)} %convert_add_fusion, f32[18,4]{1,0:T(8,128)S(1)} %fusion.81), kind=kOutput, calls=%fused_computation.1 | convolution fusion | flops 231211008 | bytes 5243168 | tf_op jit(solution)/shard_map/dot_general | solution.py:49
  68.1 0.8 iota_compare_fusion.2
  68.9 0.7 fusion.80
  69.7 3.5 %collective-permute-start.10 = (bf16[4,128,128]{2,1,0:T(8,128)(2,1)}, bf16[4,128,128]{2,1,0:T(8,128)(2,1)}, u32[]{:S(2)}, u32[]{:S(2)}) collective-permute-start(bf16[4,128,128]{2,1,0:T(8,128)(2,1)} %fusion.80), channel_id=1, source_target_pairs={{0,16},{1,17},{2,18},{3,19},{4,20},{5,21},{6,22},{7,23},{8,24},{9,... | collective-permute-start | bytes 393224 | tf_op jit(solution)/shard_map/ppermute | solution.py:17
  73.1 5.7 %fusion.4 = f32[512,4,128]{0,2,1:T(8,128)} fusion(bf16[512,4,128]{0,2,1:T(8,128)(2,1)S(1)} %bitcast.123, f32[4,512,512]{2,0,1:T(4,128)} %fusion, pred[512,512]{1,0:T(8,128)(4,1)} %iota_compare_fusion.2, bf16[512,512]{1,0:T(8,128)(2,1)} %param.7, bf16[512,512]{1,0:T(8,128)(2,1)S(1)} %copy-done.2), kind=kOutput, calls=%fused_computation.11 | convolution fusion | flops 540016640 | bytes 7077888 | tf_op jit(solution)/shard_map/hts,thd->shd/dot_general | solution.py:64
  78.8 1.1 fusion.58
  79.9 5.0 %collective-permute-start.11 = (bf16[4,128,128]{2,1,0:T(8,128)(2,1)S(1)}, bf16[4,128,128]{2,1,0:T(8,128)(2,1)S(1)}, u32[]{:S(2)}, u32[]{:S(2)}) collective-permute-start(bf16[4,128,128]{2,1,0:T(8,128)(2,1)S(1)} %fusion.58), channel_id=1, source_target_pairs={{0,32},{1,33},{2,34},{3,35},{4,36},{5,37},{6,38},{7,39},{8,40},{9,... | collective-permute-start | bytes 393224 | tf_op jit(solution)/shard_map/ppermute | solution.py:17
  85.0 3.3 %collective-permute-done.11 = bf16[4,128,128]{2,1,0:T(8,128)(2,1)S(1)} collective-permute-done((bf16[4,128,128]{2,1,0:T(8,128)(2,1)S(1)}, bf16[4,128,128]{2,1,0:T(8,128)(2,1)S(1)}, u32[]{:S(2)}, u32[]{:S(2)}) %collective-permute-start.11) | collective-permute-done | bytes 131104 | tf_op jit(solution)/shard_map/ppermute | solution.py:17
  88.3 0.7 copy-done.15
  88.9 2.0 fusion.10
  90.9 0.8 copy-done.9
  91.7 2.6 fusion.2
  94.4 1.4 convolution_convert_fusion.2
  95.8 6.7 %collective-permute-start = (bf16[4,128,128]{2,1,0:T(8,128)(2,1)S(1)}, bf16[4,128,128]{2,1,0:T(8,128)(2,1)S(1)}, u32[]{:S(2)}, u32[]{:S(2)}) collective-permute-start(bf16[4,128,128]{2,1,0:T(8,128)(2,1)S(1)} %convolution_convert_fusion.2), channel_id=1, source_target_pairs={{0,1},{1,0},{2,3},{3,2},{4,5},{5,4},{6,7},{7,6},{8,9},{9,8},{10,11... | collective-permute-start | bytes 393224 | tf_op jit(solution)/shard_map/ppermute | solution.py:17
  102.6 2.9 collective-permute-done
  105.5 1.9 collective-permute-start.1
  107.5 5.9 %collective-permute-done.1 = bf16[4,128,128]{2,1,0:T(8,128)(2,1)S(1)} collective-permute-done((bf16[4,128,128]{2,1,0:T(8,128)(2,1)S(1)}, bf16[4,128,128]{2,1,0:T(8,128)(2,1)S(1)}, u32[]{:S(2)}, u32[]{:S(2)}) %collective-permute-start.1) | collective-permute-done | bytes 131104 | tf_op jit(solution)/shard_map/ppermute | solution.py:17
  113.5 6.9 %collective-permute-start.2 = (bf16[4,128,128]{2,1,0:T(8,128)(2,1)S(1)}, bf16[4,128,128]{2,1,0:T(8,128)(2,1)S(1)}, u32[]{:S(2)}, u32[]{:S(2)}) collective-permute-start(bf16[4,128,128]{2,1,0:T(8,128)(2,1)S(1)} %fusion.85), channel_id=1, source_target_pairs={{0,4},{1,5},{2,6},{3,7},{4,0},{5,1},{6,2},{7,3},{8,12},{9,13},{10,... | collective-permute-start | bytes 393224 | tf_op jit(solution)/shard_map/ppermute | solution.py:17
  120.3 4.2 %multiply_convert_fusion.1 = bf16[4,512,512]{2,1,0:T(8,128)(2,1)S(1)} fusion(f32[4,512,512]{2,0,1:T(4,128)} %fusion, bf16[512,4,128]{0,2,1:T(8,128)(2,1)S(1)} %bitcast.124, pred[512,512]{1,0:T(8,128)(4,1)} %iota_compare_fusion.2, bf16[512,512]{1,0:T(8,128)(2,1)} %param.9), kind=kOutput, calls=%fused_computation.5 | convolution fusion | flops 271581184 | bytes 7602176 | tf_op jit(solution)/shard_map/thd,shd->hts/dot_general | solution.py:65
  124.5 2.7 collective-permute-done.2
  127.3 5.5 %collective-permute-start.3 = (bf16[4,128,128]{2,1,0:T(8,128)(2,1)S(1)}, bf16[4,128,128]{2,1,0:T(8,128)(2,1)S(1)}, u32[]{:S(2)}, u32[]{:S(2)}) collective-permute-start(bf16[4,128,128]{2,1,0:T(8,128)(2,1)S(1)} %fusion.63), channel_id=1, source_target_pairs={{0,8},{1,9},{2,10},{3,11},{4,12},{5,13},{6,14},{7,15},{8,0},{9,1},... | collective-permute-start | bytes 393224 | tf_op jit(solution)/shard_map/ppermute | solution.py:17
  132.8 1.5 convolution_bitcast_fusion
  134.3 9.1 %collective-permute-done.3 = bf16[4,128,128]{2,1,0:T(8,128)(2,1)S(1)} collective-permute-done((bf16[4,128,128]{2,1,0:T(8,128)(2,1)S(1)}, bf16[4,128,128]{2,1,0:T(8,128)(2,1)S(1)}, u32[]{:S(2)}, u32[]{:S(2)}) %collective-permute-start.3) | collective-permute-done | bytes 131104 | tf_op jit(solution)/shard_map/ppermute | solution.py:17
  143.4 0.7 fusion.79
  144.2 2.4 collective-permute-start.4
  146.6 2.0 copy.108
  148.7 3.4 %convolution_bitcast_fusion.1 = f32[512,4,128]{0,2,1:T(8,128)} fusion(bf16[4,512,512]{2,1,0:T(8,128)(2,1)} %copy-done.1, bf16[512,512]{1,0:T(8,128)(2,1)S(1)} %copy-done.2), kind=kOutput, calls=%fused_computation.10 | convolution fusion | flops 268435456 | bytes 3670016 | tf_op jit(solution)/shard_map/hts,shd->thd/dot_general | solution.py:67
  152.1 1.4 dynamic-slice
  153.4 1.2 dynamic-slice.1
  154.7 1.3 dynamic-slice.2
  155.9 1.3 dynamic-slice.3
  157.2 1.7 copy.100
  158.9 1.4 fusion.46
  160.3 5.1 %collective-permute-start.5 = (bf16[4,128,128]{2,1,0:T(8,128)(2,1)S(1)}, bf16[4,128,128]{2,1,0:T(8,128)(2,1)S(1)}, u32[]{:S(2)}, u32[]{:S(2)}) collective-permute-start(bf16[4,128,128]{2,1,0:T(8,128)(2,1)S(1)} %fusion.46), channel_id=1, source_target_pairs={{0,32},{1,33},{2,34},{3,35},{4,36},{5,37},{6,38},{7,39},{8,40},{9,... | collective-permute-start | bytes 393224 | tf_op jit(solution)/shard_map/ppermute | solution.py:17
  165.4 2.9 fusion.9
  168.7 2.2 fusion.8
  170.8 51.5 %reduce-scatter.7.cloned.1.call-done = bf16[32,512]{1,0:T(8,128)(2,1)} async-done(((bf16[512,512]{1,0:T(8,128)(2,1)}), bf16[32,512]{1,0:T(8,128)(2,1)}) %reduce-scatter.7.cloned.1.call-update) | async-done | bytes 32784
  222.3 0.9 copy.109
  223.2 0.7 fusion.59
  223.8 1.4 dynamic-update-slice
  225.3 2.0 copy.103
  227.3 10.5 %all-reduce = f32[4]{0:T(128)S(1)} all-reduce(f32[4]{0:T(128)S(1)} %dynamic-update-slice), channel_id=1, replica_groups=mesh['head_0'=4,'head_1'=2,'seq_0'=4,'seq_1'=16] {'head_0'}, use_global_device_ids=true, to_apply=%add | all-reduce | flops 4 | bytes 32
  238.4 1.3 dynamic-update-slice.1
  239.7 2.0 copy.102
  241.7 2.4 all-reduce.1
  244.8 1.3 dynamic-update-slice.2
  246.1 2.0 copy.101
  248.2 10.3 %all-reduce.2 = f32[4]{0:T(128)S(1)} all-reduce(f32[4]{0:T(128)S(1)} %dynamic-update-slice.2), channel_id=1, replica_groups=mesh['head_0'=4,'head_1'=2,'seq_0'=4,'seq_1'=16] {'seq_0'}, use_global_device_ids=true, to_apply=%add.2 | all-reduce | flops 4 | bytes 32
  259.1 1.4 dynamic-update-slice.3
  260.5 28.1 %all-reduce.3 = f32[16]{0:T(128)S(1)} all-reduce(f32[16]{0:T(128)S(1)} %dynamic-update-slice.3), channel_id=1, replica_groups=mesh['head_0'=4,'head_1'=2,'seq_0'=4,'seq_1'=16] {'seq_1'}, use_global_device_ids=true, to_apply=%add.3 | all-reduce | flops 16 | bytes 128
  289.8 1.0 fusion.60
  290.8 0.7 copy.104
  (70 shorter events, 3.3 us)
Async XLA Ops:
  7.2 84.6 %copy-start = (bf16[512,2048]{1,0:T(8,128)(2,1)S(1)}, bf16[512,2048]{1,0:T(8,128)(2,1)}, u32[]{:S(2)}) copy-start(bf16[512,2048]{1,0:T(8,128)(2,1)} %param.11) | copy-start | bytes 6291460
  7.2 139.4 %reduce-scatter.5.cloned.1.call-start = ((), (), s32[]{:S(2)}) async-start(), calls=%async_computation.2 | async-start | bytes 2621440 | tf_op jit(solution)/shard_map/reduce_scatter | solution.py:23
  10.0 10.3 %collective-permute-start.6 = (bf16[4,128,128]{2,1,0:T(8,128)(2,1)S(1)}, bf16[4,128,128]{2,1,0:T(8,128)(2,1)S(1)}, u32[]{:S(2)}, u32[]{:S(2)}) collective-permute-start(bf16[4,128,128]{2,1,0:T(8,128)(2,1)S(1)} %convolution_convert_fusion.1), channel_id=1, source_target_pairs={{0,1},{1,0},{2,3},{3,2},{4,5},{5,4},{6,7},{7,6},{8,9},{9,8},{10,11... | collective-permute-start | bytes 393224 | tf_op jit(solution)/shard_map/ppermute | solution.py:17
  21.0 8.1 %collective-permute-start.7 = (bf16[4,128,128]{2,1,0:T(8,128)(2,1)}, bf16[4,128,128]{2,1,0:T(8,128)(2,1)S(1)}, u32[]{:S(2)}, u32[]{:S(2)}) collective-permute-start(bf16[4,128,128]{2,1,0:T(8,128)(2,1)} %fusion.62), channel_id=1, source_target_pairs={{0,2},{1,3},{2,0},{3,1},{4,6},{5,7},{6,4},{7,5},{8,10},{9,11},{10,... | collective-permute-start | bytes 393224 | tf_op jit(solution)/shard_map/ppermute | solution.py:17
  26.3 46.8 %copy-start.2 = (bf16[512,512]{1,0:T(8,128)(2,1)S(1)}, bf16[512,512]{1,0:T(8,128)(2,1)}, u32[]{:S(2)}) copy-start(bf16[512,512]{1,0:T(8,128)(2,1)} %param.8) | copy-start | bytes 1572868
  29.2 15.5 %collective-permute-start.8 = (bf16[4,128,128]{2,1,0:T(8,128)(2,1)S(1)}, bf16[4,128,128]{2,1,0:T(8,128)(2,1)S(1)}, u32[]{:S(2)}, u32[]{:S(2)}) collective-permute-start(bf16[4,128,128]{2,1,0:T(8,128)(2,1)S(1)} %fusion.86), channel_id=1, source_target_pairs={{0,4},{1,5},{2,6},{3,7},{4,0},{5,1},{6,2},{7,3},{8,12},{9,13},{10,... | collective-permute-start | bytes 393224 | tf_op jit(solution)/shard_map/ppermute | solution.py:17
  44.6 24.3 %copy-start.5 = (bf16[4,128,128]{2,1,0:T(8,128)(2,1)}, bf16[4,128,128]{2,1,0:T(8,128)(2,1)S(1)}, u32[]{:S(2)}) copy-start(bf16[4,128,128]{2,1,0:T(8,128)(2,1)S(1)} %collective-permute-done.8) | copy-start | bytes 393220
  44.7 24.2 %collective-permute-start.9 = (bf16[4,128,128]{2,1,0:T(8,128)(2,1)S(1)}, bf16[4,128,128]{2,1,0:T(8,128)(2,1)S(1)}, u32[]{:S(2)}, u32[]{:S(2)}) collective-permute-start(bf16[4,128,128]{2,1,0:T(8,128)(2,1)S(1)} %fusion.64), channel_id=1, source_target_pairs={{0,8},{1,9},{2,10},{3,11},{4,12},{5,13},{6,14},{7,15},{8,0},{9,1},... | collective-permute-start | bytes 393224 | tf_op jit(solution)/shard_map/ppermute | solution.py:17
  68.9 0.8 copy-start.10
  69.7 9.1 %collective-permute-start.10 = (bf16[4,128,128]{2,1,0:T(8,128)(2,1)}, bf16[4,128,128]{2,1,0:T(8,128)(2,1)}, u32[]{:S(2)}, u32[]{:S(2)}) collective-permute-start(bf16[4,128,128]{2,1,0:T(8,128)(2,1)} %fusion.80), channel_id=1, source_target_pairs={{0,16},{1,17},{2,18},{3,19},{4,20},{5,21},{6,22},{7,23},{8,24},{9,... | collective-permute-start | bytes 393224 | tf_op jit(solution)/shard_map/ppermute | solution.py:17
  79.9 8.4 %collective-permute-start.11 = (bf16[4,128,128]{2,1,0:T(8,128)(2,1)S(1)}, bf16[4,128,128]{2,1,0:T(8,128)(2,1)S(1)}, u32[]{:S(2)}, u32[]{:S(2)}) collective-permute-start(bf16[4,128,128]{2,1,0:T(8,128)(2,1)S(1)} %fusion.58), channel_id=1, source_target_pairs={{0,32},{1,33},{2,34},{3,35},{4,36},{5,37},{6,38},{7,39},{8,40},{9,... | collective-permute-start | bytes 393224 | tf_op jit(solution)/shard_map/ppermute | solution.py:17
  84.9 9.4 %copy-start.16 = (f32[4]{0:T(128)}, f32[4]{0:T(128)S(1)}, u32[]{:S(2)}) copy-start(f32[4]{0:T(128)S(1)} %get-tuple-element.21) | copy-start | bytes 52
  85.0 9.4 %copy-start.18 = (f32[4]{0:T(128)}, f32[4]{0:T(128)S(1)}, u32[]{:S(2)}) copy-start(f32[4]{0:T(128)S(1)} %get-tuple-element.22) | copy-start | bytes 52
  85.0 9.3 %copy-start.20 = (f32[4]{0:T(128)}, f32[4]{0:T(128)S(1)}, u32[]{:S(2)}) copy-start(f32[4]{0:T(128)S(1)} %get-tuple-element.23) | copy-start | bytes 52
  85.0 9.3 %copy-start.22 = (f32[4]{0:T(128)}, f32[4]{0:T(128)S(1)}, u32[]{:S(2)}) copy-start(f32[4]{0:T(128)S(1)} %get-tuple-element.24) | copy-start | bytes 52
  85.0 9.3 %copy-start.23 = (f32[4]{0:T(128)}, f32[4]{0:T(128)S(1)}, u32[]{:S(2)}) copy-start(f32[4]{0:T(128)S(1)} %get-tuple-element.25) | copy-start | bytes 52
  88.3 0.7 copy-start.15
  90.9 0.8 copy-start.9
  94.4 127.9 %reduce-scatter.7.cloned.1.call-start = ((), (), s32[]{:S(2)}) async-start(), calls=%async_computation.3 | async-start | bytes 557056
  95.8 47.6 %copy-start.8 = (bf16[4,128,128]{2,1,0:T(8,128)(2,1)}, bf16[4,128,128]{2,1,0:T(8,128)(2,1)S(1)}, u32[]{:S(2)}) copy-start(bf16[4,128,128]{2,1,0:T(8,128)(2,1)S(1)} %convolution_convert_fusion.2) | copy-start | bytes 393220
  95.8 9.7 %collective-permute-start = (bf16[4,128,128]{2,1,0:T(8,128)(2,1)S(1)}, bf16[4,128,128]{2,1,0:T(8,128)(2,1)S(1)}, u32[]{:S(2)}, u32[]{:S(2)}) collective-permute-start(bf16[4,128,128]{2,1,0:T(8,128)(2,1)S(1)} %convolution_convert_fusion.2), channel_id=1, source_target_pairs={{0,1},{1,0},{2,3},{3,2},{4,5},{5,4},{6,7},{7,6},{8,9},{9,8},{10,11... | collective-permute-start | bytes 393224 | tf_op jit(solution)/shard_map/ppermute | solution.py:17
  105.5 7.9 %collective-permute-start.1 = (bf16[4,128,128]{2,1,0:T(8,128)(2,1)S(1)}, bf16[4,128,128]{2,1,0:T(8,128)(2,1)S(1)}, u32[]{:S(2)}, u32[]{:S(2)}) collective-permute-start(bf16[4,128,128]{2,1,0:T(8,128)(2,1)S(1)} %fusion.61), channel_id=1, source_target_pairs={{0,2},{1,3},{2,0},{3,1},{4,6},{5,7},{6,4},{7,5},{8,10},{9,11},{10,... | collective-permute-start | bytes 393224 | tf_op jit(solution)/shard_map/ppermute | solution.py:17
  113.4 30.0 %copy-start.6 = (bf16[4,128,128]{2,1,0:T(8,128)(2,1)}, bf16[4,128,128]{2,1,0:T(8,128)(2,1)S(1)}, u32[]{:S(2)}) copy-start(bf16[4,128,128]{2,1,0:T(8,128)(2,1)S(1)} %collective-permute-done.1) | copy-start | bytes 393220
  113.5 19.3 %copy-start.3 = (bf16[512,512]{1,0:T(8,128)(2,1)S(1)}, bf16[512,512]{1,0:T(8,128)(2,1)}, u32[]{:S(2)}) copy-start(bf16[512,512]{1,0:T(8,128)(2,1)} %param.7) | copy-start | bytes 1572868
  113.5 13.7 %collective-permute-start.2 = (bf16[4,128,128]{2,1,0:T(8,128)(2,1)S(1)}, bf16[4,128,128]{2,1,0:T(8,128)(2,1)S(1)}, u32[]{:S(2)}, u32[]{:S(2)}) collective-permute-start(bf16[4,128,128]{2,1,0:T(8,128)(2,1)S(1)} %fusion.85), channel_id=1, source_target_pairs={{0,4},{1,5},{2,6},{3,7},{4,0},{5,1},{6,2},{7,3},{8,12},{9,13},{10,... | collective-permute-start | bytes 393224 | tf_op jit(solution)/shard_map/ppermute | solution.py:17
  124.5 8.3 %copy-start.1 = (bf16[4,512,512]{2,1,0:T(8,128)(2,1)}, bf16[4,512,512]{2,1,0:T(8,128)(2,1)S(1)}, u32[]{:S(2)}) copy-start(bf16[4,512,512]{2,1,0:T(8,128)(2,1)S(1)} %multiply_convert_fusion.1) | copy-start | bytes 6291460
  127.2 17.0 %copy-start.11 = (bf16[4,128,128]{2,1,0:T(8,128)(2,1)}, bf16[4,128,128]{2,1,0:T(8,128)(2,1)S(1)}, u32[]{:S(2)}) copy-start(bf16[4,128,128]{2,1,0:T(8,128)(2,1)S(1)} %collective-permute-done.2) | copy-start | bytes 393220
  127.3 16.1 %collective-permute-start.3 = (bf16[4,128,128]{2,1,0:T(8,128)(2,1)S(1)}, bf16[4,128,128]{2,1,0:T(8,128)(2,1)S(1)}, u32[]{:S(2)}, u32[]{:S(2)}) collective-permute-start(bf16[4,128,128]{2,1,0:T(8,128)(2,1)S(1)} %fusion.63), channel_id=1, source_target_pairs={{0,8},{1,9},{2,10},{3,11},{4,12},{5,13},{6,14},{7,15},{8,0},{9,1},... | collective-permute-start | bytes 393224 | tf_op jit(solution)/shard_map/ppermute | solution.py:17
  134.3 31.1 %copy-start.17 = (f32[4]{0:T(128)S(1)}, f32[4]{0:T(128)}, u32[]{:S(2)}) copy-start(f32[4]{0:T(128)} %copy-done.16) | copy-start | bytes 52
  134.3 31.1 %copy-start.19 = (f32[4]{0:T(128)S(1)}, f32[4]{0:T(128)}, u32[]{:S(2)}) copy-start(f32[4]{0:T(128)} %copy-done.18) | copy-start | bytes 52
  134.3 31.1 %copy-start.21 = (f32[4]{0:T(128)S(1)}, f32[4]{0:T(128)}, u32[]{:S(2)}) copy-start(f32[4]{0:T(128)} %copy-done.20) | copy-start | bytes 52
  143.4 0.8 copy-start.13
  144.2 14.8 %collective-permute-start.4 = (bf16[4,128,128]{2,1,0:T(8,128)(2,1)}, bf16[4,128,128]{2,1,0:T(8,128)(2,1)}, u32[]{:S(2)}, u32[]{:S(2)}) collective-permute-start(bf16[4,128,128]{2,1,0:T(8,128)(2,1)} %fusion.79), channel_id=1, source_target_pairs={{0,16},{1,17},{2,18},{3,19},{4,20},{5,21},{6,22},{7,23},{8,24},{9,... | collective-permute-start | bytes 393224 | tf_op jit(solution)/shard_map/ppermute | solution.py:17
  152.1 16.6 %copy-start.7 = (bf16[4,128,128]{2,1,0:T(8,128)(2,1)S(1)}, bf16[4,128,128]{2,1,0:T(8,128)(2,1)}, u32[]{:S(2)}) copy-start(bf16[4,128,128]{2,1,0:T(8,128)(2,1)} %copy-done.6) | copy-start | bytes 393220
  152.1 16.6 %copy-start.12 = (bf16[4,128,128]{2,1,0:T(8,128)(2,1)S(1)}, bf16[4,128,128]{2,1,0:T(8,128)(2,1)}, u32[]{:S(2)}) copy-start(bf16[4,128,128]{2,1,0:T(8,128)(2,1)} %copy-done.11) | copy-start | bytes 393220
  152.1 16.6 %copy-start.14 = (bf16[4,128,128]{2,1,0:T(8,128)(2,1)S(1)}, bf16[4,128,128]{2,1,0:T(8,128)(2,1)}, u32[]{:S(2)}) copy-start(bf16[4,128,128]{2,1,0:T(8,128)(2,1)} %copy-done.13) | copy-start | bytes 393220
  158.9 9.7 %copy-start.4 = (f32[512,4,128]{0,2,1:T(8,128)S(1)}, f32[512,4,128]{0,2,1:T(8,128)}, u32[]{:S(2)}) copy-start(f32[512,4,128]{0,2,1:T(8,128)} %convolution_bitcast_fusion.1) | copy-start | bytes 3145732
  160.3 8.4 %collective-permute-start.5 = (bf16[4,128,128]{2,1,0:T(8,128)(2,1)S(1)}, bf16[4,128,128]{2,1,0:T(8,128)(2,1)S(1)}, u32[]{:S(2)}, u32[]{:S(2)}) collective-permute-start(bf16[4,128,128]{2,1,0:T(8,128)(2,1)S(1)} %fusion.46), channel_id=1, source_target_pairs={{0,32},{1,33},{2,34},{3,35},{4,36},{5,37},{6,38},{7,39},{8,40},{9,... | collective-permute-start | bytes 393224 | tf_op jit(solution)/shard_map/ppermute | solution.py:17
Sparse Core Ops, SparseCore 0:
  94.5 38.4 reduce-scatter.4
  148.8 73.4 reduce-scatter.6
